TPU v7x, 512 devices: a whole 4x4x16 slice. The times are simulated.
512 devices in a mesh: chan: 64 (over x, y, z_hi, core), seg: 8 (over z_lo).
Axes of the slice: x: 4, y: 4, z: 16 (z_hi: 2, z_lo: 8; z = z_hi * 8 + z_lo), core: 2. Of those that a mesh axis runs over, the one named last changes fastest.
Arguments:
- records: bfloat16 [8, 16384, 4, 512], P('seg', 'chan'), may hold values from -6 to 6
- alive: int32 [16384], P('chan'), may hold values 0 or 1
- offsets: int32 [64, 16], P('chan'), may hold values from 1 to 256, as said below
Outputs:
- correlations: bfloat16 [16, 16384, 256], P('seg', 'chan')
Inputs may be any that keep to these rules, and one draw needn't show every extreme that they name: Each block's 16 offsets are distinct and one of them is 256.
All inputs are finite; a program needn't handle non-finite values. No bound on the sum of `alive` on one device may be relied on, other than what follows from the above.
Results may differ from a plain program's by a relative error of at most 0.02.
Values may be sent and summed in bfloat16 or wider, within the bound.
A program may use at most 64 MiB of HBM per device.

v0:
```python
import jax
import jax.numpy as jnp
from jax import lax
from jax.sharding import PartitionSpec as P

W = 4
WIN = 512
NF = 128
F0 = 1
NL = 256
K = 16


eps = 1e-06


def shifted(shard, axis, by):
    size = lax.axis_size(axis)
    pairs = [(i, i + by) for i in range(size) if 0 <= i + by < size]
    return lax.ppermute(shard, axis, pairs)


def forward_table():
    times = jnp.arange(WIN, dtype=jnp.int32)[:, None]
    bins = F0 + jnp.arange(NF, dtype=jnp.int32)[None, :]
    angle = (times * bins % WIN).astype(jnp.float32) * (2.0 * jnp.pi / WIN)
    return jnp.concatenate([jnp.cos(angle), -jnp.sin(angle)], axis=1).astype(jnp.bfloat16)


def lag_table():
    bins = F0 + jnp.arange(NF, dtype=jnp.int32)[:, None]
    lags = jnp.arange(NL, dtype=jnp.int32)[None, :] - NL // 2
    angle = (bins * lags % WIN).astype(jnp.float32) * (2.0 * jnp.pi / WIN)
    return jnp.concatenate([jnp.cos(angle), -jnp.sin(angle)], axis=0) / NF


def whiten(raw, live, table):
    count = raw.shape[0]
    spectra = jnp.dot(raw.reshape(count * W, WIN), table, preferred_element_type=jnp.float32)
    spectra = spectra.reshape(count, W, 2 * NF)
    power = jnp.mean(spectra * spectra, axis=-1, keepdims=True)
    scaled = spectra * lax.rsqrt(power + eps) * live.astype(jnp.float32)[:, None, None]
    return scaled.astype(jnp.bfloat16)


def pair_product(first, second):
    second = second.astype(jnp.float32)
    first_re, first_im = (first[..., :NF], first[..., NF:])
    second_re, second_im = (second[..., :NF], second[..., NF:])
    real_part = jnp.sum(first_re * second_re + first_im * second_im, axis=1)
    imag_part = jnp.sum(first_im * second_re - first_re * second_im, axis=1)
    return jnp.concatenate([real_part, imag_part], axis=-1)


def shards(records, alive, offsets):
    table = forward_table()
    local_raw = records[0]
    live_flags = alive.astype(jnp.bfloat16)
    own = whiten(local_raw, live_flags, table)
    rim_raw, rim_live = shifted((local_raw, live_flags), "chan", -1)
    rim = whiten(rim_raw, rim_live, table)
    extended = jnp.concatenate([own, rim], axis=0)
    own_wide = own.astype(jnp.float32)
    count = own.shape[0]

    def one_slot(slot):
        start = offsets[0, slot]
        partner = lax.dynamic_slice_in_dim(extended, start, count, 0)
        return pair_product(own_wide, partner)

    terms = lax.map(one_slot, jnp.arange(K, dtype=jnp.int32))
    total = lax.psum(terms.astype(jnp.bfloat16), "seg").astype(jnp.float32)
    share = K // lax.axis_size("seg")
    mine = lax.dynamic_slice_in_dim(total, lax.axis_index("seg") * share, share, 0)
    result = jnp.einsum("kcf,fl->kcl", mine, lag_table(), precision=lax.Precision.HIGHEST)
    return result.astype(jnp.bfloat16)


def solution(mesh):
    in_specs = (P("seg", "chan", None, None), P("chan"), P("chan", None))
    out_specs = P("seg", "chan", None)
    return jax.shard_map(shards, mesh=mesh, in_specs=in_specs, out_specs=out_specs, check_vma=False)
```

profile of v0, /device:TPU:1, one launch (start us, length us, event | category | flops | bytes accessed | tf_op | source)
XLA Modules:
  0.0 323.8 jit_solution(13814156537339358147)
XLA Ops:
  6.5 8.8 %collective-permute-start = (bf16[256,4,512]{2,1,0:T(4,128)(2,1)}, bf16[256,4,512]{2,1,0:T(4,128)(2,1)}, u32[]{:S(2)}, u32[]{:S(2)}) collective-permute-start(bf16[256,4,512]{2,1,0:T(4,128)(2,1)} %bitcast.22), channel_id=1, source_target_pairs={{8,0},{16,8},{24,16},{32,24},{40,32},{48,40},{56,48},{64,56},{72,6... | collective-permute-start | bytes 3145736 | tf_op jit(solution)/shard_map/ppermute | solution.py:20
  15.3 0.7 fusion.23
  16.0 1.9 collective-permute-start.1
  17.9 1.3 reshape_squeeze.3
  19.3 1.1 cosine_convert_fusion
  21.7 1.6 fusion.22
  23.3 13.1 %collective-permute-done.1 = bf16[256]{0:T(256)(128)(2,1)S(1)} collective-permute-done((bf16[256]{0:T(256)(128)(2,1)S(1)}, bf16[256]{0:T(256)(128)(2,1)S(1)}, u32[]{:S(2)}, u32[]{:S(2)}) %collective-permute-start.1) | collective-permute-done | bytes 544 | tf_op jit(solution)/shard_map/ppermute | solution.py:20
  36.5 1.3 reshape.61
  39.1 0.9 multiply_convert_fusion
  40.0 0.7 pad_maximum_fusion
  40.7 103.7 %while.10 = (s32[]{:T(128)}, bf16[16,256,256]{2,1,0:T(8,128)(2,1)}, f32[256,4,256]{2,1,0:T(4,128)S(1)}, s32[16]{0:T(128)S(1)}, s32[1,16]{1,0:T(1,128)S(1)}, /*in...) while((s32[]{:T(128)}, bf16[16,256,256]{2,1,0:T(8,128)(2,1)}, ...), condition=%wide.region_5.6_spmd, body=%wide.region_2.5_spmd.sunk | while | flops 1507336 | bytes 4063941 | solution.py:71
  40.7 0.6 dynamic_slice.23
  43.2 0.6 constant_dynamic-slice_fusion.2
  45.8 0.8 add_reduce_fusion.2
  46.5 0.7 fusion.27
  49.7 0.6 constant_dynamic-slice_fusion.2
  52.2 0.8 add_reduce_fusion.2
  53.0 0.7 fusion.27
  58.7 0.8 add_reduce_fusion.2
  59.5 0.7 fusion.27
  65.2 0.8 add_reduce_fusion.2
  66.0 0.7 fusion.27
  71.7 0.8 add_reduce_fusion.2
  72.4 0.7 fusion.27
  78.1 0.8 add_reduce_fusion.2
  78.9 0.7 fusion.27
  84.6 0.8 add_reduce_fusion.2
  85.4 0.7 fusion.27
  91.1 0.8 add_reduce_fusion.2
  91.9 0.7 fusion.27
  97.6 0.8 add_reduce_fusion.2
  98.4 0.7 fusion.27
  104.1 0.8 add_reduce_fusion.2
  104.8 0.7 fusion.27
  110.5 0.8 add_reduce_fusion.2
  111.3 0.7 fusion.27
  117.0 0.8 add_reduce_fusion.2
  117.8 0.7 fusion.27
  123.5 0.8 add_reduce_fusion.2
  124.3 0.7 fusion.27
  130.0 0.8 add_reduce_fusion.2
  130.7 0.7 fusion.27
  136.5 0.8 add_reduce_fusion.2
  137.2 0.7 fusion.27
  142.9 0.8 add_reduce_fusion.2
  143.7 0.7 fusion.27
  145.0 169.9 %all-reduce.2.cloned.1.call-done = bf16[16,256,256]{2,1,0:T(8,128)(2,1)} async-done(((bf16[16,256,256]{2,1,0:T(8,128)(2,1)}), bf16[16,256,256]{2,1,0:T(8,128)(2,1)}) %all-reduce.2.cloned.1.call-update) | async-done | bytes 2097168 | tf_op jit(solution)/shard_map/psum | solution.py:72
  314.9 2.1 convolution_convert_fusion
  (68 shorter events, 23.3 us)
Async XLA Ops:
  6.5 308.4 %all-reduce.2.cloned.1.call-start = ((), (), s32[]{:S(2)}) async-start(), calls=%async_computation | async-start | bytes 4194304 | tf_op jit(solution)/shard_map/psum | solution.py:72
  6.5 29.9 %collective-permute-start = (bf16[256,4,512]{2,1,0:T(4,128)(2,1)}, bf16[256,4,512]{2,1,0:T(4,128)(2,1)}, u32[]{:S(2)}, u32[]{:S(2)}) collective-permute-start(bf16[256,4,512]{2,1,0:T(4,128)(2,1)} %bitcast.22), channel_id=1, source_target_pairs={{8,0},{16,8},{24,16},{32,24},{40,32},{48,40},{56,48},{64,56},{72,6... | collective-permute-start | bytes 3145736 | tf_op jit(solution)/shard_map/ppermute | solution.py:20
  16.0 20.4 %collective-permute-start.1 = (bf16[256]{0:T(256)(128)(2,1)S(1)}, bf16[256]{0:T(256)(128)(2,1)S(1)}, u32[]{:S(2)}, u32[]{:S(2)}) collective-permute-start(bf16[256]{0:T(256)(128)(2,1)S(1)} %get-tuple-element.55), channel_id=1, source_target_pairs={{8,0},{16,8},{24,16},{32,24},{40,32},{48,40},{56,48},{64,56},{72,6... | collective-permute-start | bytes 1544 | tf_op jit(solution)/shard_map/ppermute | solution.py:20
  39.0 1.0 copy-start
  39.0 1.7 copy-start.1
Sparse Core Ops, SparseCore 0:
  144.5 170.3 all-reduce.1
where the time goes:
time: 329 us; the launch traced here: 324 us
  waiting for transfers between devices  183 us (56%)
  loops' own time  58.7 us (18%)
  other arithmetic  30.8 us (9%)
  local copies, waits for them, and re-layouts  23.9 us (7%)
  between operations  13.6 us (4%)
  starting transfers between devices  10.7 us (3%)
    psum x1, waiting for transfers between devices, shards(): total = lax.psum(terms.astype(jnp.bfloat16), 'seg').astype(jnp.float32)  170 us
    another operation x1, loops' own time, shards(): terms = lax.map(one_slot, jnp.arange(K, dtype=jnp.int32))  58.7 us
    ppermute x2, waiting for transfers between devices, shifted(): return lax.ppermute(shard, axis, pairs)  13.1 us
    reduce_sum x16, other arithmetic, pair_product(): real_part = jnp.sum(first_re * second_re + first_im * second_im, axis=1)  12.2 us
    dynamic_update_slice x16, other arithmetic, shards(): terms = lax.map(one_slot, jnp.arange(K, dtype=jnp.int32))  10.8 us
    ppermute x2, starting transfers between devices, shifted(): return lax.ppermute(shard, axis, pairs)  10.7 us
    dynamic_slice x16, local copies, waits for them, and re-layouts, one_slot(): start = offsets[0, slot]  9.86 us
    dynamic_slice x16, local copies, waits for them, and re-layouts, shards(): terms = lax.map(one_slot, jnp.arange(K, dtype=jnp.int32))  9.81 us
  transfers between devices with their start and end apart: 3, of which 2 were waited for; matrix products, arithmetic and copies ran while one was open for 2% of the time, Pallas kernels for 0%

commit v1 on v0

v1 whole, which is shorter than its diff:
```python
import functools

import jax
import jax.numpy as jnp
import numpy as np
from jax import lax
from jax.experimental import pallas as pl
from jax.experimental.pallas import tpu as pltpu
from jax.sharding import PartitionSpec as P

W = 4
WIN = 512
NF = 128
F0 = 1
NL = 256
K = 16
C = 256
SEGS = 8
CHIPS = 16
BINS = NF // CHIPS
PHASES = 2
LANES = 128
eps = 1e-06
MESH = pl.DeviceIdType.MESH


def bin_order():
    chip, part, which = np.meshgrid(np.arange(CHIPS), np.arange(2), np.arange(BINS), indexing="ij")
    return (F0 + chip * BINS + which).reshape(-1), part.reshape(-1)


def forward_table():
    bins, part = bin_order()
    turn = (bins[:, None] * np.arange(WIN)[None, :]) % WIN
    angle = turn * (2.0 * np.pi / WIN)
    rows = np.where(part[:, None] == 0, np.cos(angle), -np.sin(angle))
    return jnp.asarray(rows.astype(np.float32)).astype(jnp.bfloat16)


def lag_table():
    bins, part = bin_order()
    turn = (bins[:, None] * (np.arange(NL)[None, :] - NL // 2)) % WIN
    angle = turn * (2.0 * np.pi / WIN)
    rows = np.where(part[:, None] == 0, np.cos(angle), -np.sin(angle)) / NF
    return jnp.asarray(rows.astype(np.float32))


def kernel(columns, rec_ref, alive_ref, off_ref, tab_ref, lag_ref, out_ref,
           send, recv, rim, wide, totals, res_send, res_recv, off_src, off_recv, off_smem,
           send_sem, recv_sem, rim_send_sem, rim_recv_sem, res_send_sem, res_recv_sem,
           off_send_sem, off_recv_sem, off_local_sem):
    chan = lax.axis_index("chan")
    seg = lax.axis_index("seg")
    core = chan % 2
    zh = (chan // 2) % 2
    col = chan // 4
    z = zh * SEGS + seg
    chain = col * 2 + core
    chains = columns * 2
    before = (chain + chains - 1) % chains
    after = (chain + 1) % chains

    def on_line(chip, which):
        return ((col * 2 + chip // SEGS) * 2 + which, chip % SEGS)

    def on_chain(link):
        return (((link // 2) * 2 + zh) * 2 + link % 2, seg)

    barrier = pltpu.get_barrier_semaphore()

    def greet(t, _):
        chip = (z + t) % CHIPS

        @pl.when(jnp.logical_or(chip != z, zh != core))
        def _():
            pl.semaphore_signal(barrier, 1, device_id=on_line(chip, zh), device_id_type=MESH)
        which = t % 2
        other = core * SEGS + t // 2

        @pl.when(jnp.logical_or(other != z, which != core))
        def _():
            pl.semaphore_signal(barrier, 1, device_id=on_line(other, which), device_id_type=MESH)
        return 0

    lax.fori_loop(0, 2 * SEGS, greet, 0)
    for link in (before, after):
        pl.semaphore_signal(barrier, 1, device_id=on_chain(link), device_id_type=MESH)

    off_src[...] = jnp.zeros_like(off_src)
    off_src[0:1, 0:K] = off_ref[...]
    live = alive_ref[...].astype(jnp.float32)

    def white_copy(phase, chip):
        return pltpu.make_async_remote_copy(
            src_ref=send.at[phase, chip], dst_ref=recv.at[phase, pl.ds(core * 2, 2), seg],
            send_sem=send_sem.at[phase, chip], recv_sem=recv_sem.at[phase, core, seg],
            device_id=on_line(chip, zh), device_id_type=MESH)

    def white_local(phase):
        return pltpu.make_async_copy(
            send.at[phase, z], recv.at[phase, pl.ds(core * 2, 2), seg], recv_sem.at[phase, core, seg])

    def white_wait(phase, block, s):
        pltpu.make_async_copy(
            send.at[phase, 0], recv.at[phase, pl.ds(block * 2, 2), s], recv_sem.at[phase, block, s]).wait()

    def rim_copy(phase, s):
        return pltpu.make_async_remote_copy(
            src_ref=recv.at[phase, pl.ds(0, 2), s], dst_ref=rim.at[phase, :, s],
            send_sem=rim_send_sem.at[phase, s], recv_sem=rim_recv_sem.at[phase, s],
            device_id=on_chain(before), device_id_type=MESH)

    def off_copy(half):
        return pltpu.make_async_remote_copy(
            src_ref=off_src, dst_ref=off_recv.at[core],
            send_sem=off_send_sem.at[half], recv_sem=off_recv_sem.at[core],
            device_id=on_line(half * SEGS + seg, zh), device_id_type=MESH)

    def off_is_remote(half):
        return jnp.logical_or(half != zh, zh != core)

    for phase in range(PHASES):
        spectra = []
        for w in (2 * phase, 2 * phase + 1):
            raw = lax.dot_general(tab_ref[...], rec_ref[w], (((1,), (1,)), ((), ())),
                                  preferred_element_type=jnp.float32)
            power = jnp.sum(raw * raw, axis=0, keepdims=True) * (1.0 / (2 * NF))
            scaled = raw * (lax.rsqrt(power + eps) * live)
            spectra.append(scaled.reshape(CHIPS, 2, 1, BINS, C))
        white = jnp.concatenate(spectra, axis=2).reshape(CHIPS, 4 * BINS, C).astype(jnp.bfloat16)
        for tile in range(2):
            send[phase, :, tile] = white[:, :, tile * LANES:(tile + 1) * LANES]
        if phase == 0:
            met = 4 * SEGS + 2 - 2 * (zh == core).astype(jnp.int32)
            pl.semaphore_wait(barrier, met)
            for half in range(2):
                @pl.when(off_is_remote(half))
                def _():
                    off_copy(half).start()

                @pl.when(jnp.logical_not(off_is_remote(half)))
                def _():
                    pltpu.make_async_copy(off_src, off_recv.at[core], off_recv_sem.at[core]).start()

        def send_white(t, _):
            turn = CHIPS - 1 - t
            away = jnp.where(turn % 2 == 1, (turn + 1) // 2, CHIPS - turn // 2)
            chip = (z + away) % CHIPS

            @pl.when(jnp.logical_or(chip != z, zh != core))
            def _():
                white_copy(phase, chip).start()

            @pl.when(jnp.logical_and(chip == z, zh == core))
            def _():
                white_local(phase).start()
            return 0

        lax.fori_loop(0, CHIPS, send_white, 0)

    for block in range(2):
        pltpu.make_async_copy(off_src, off_recv.at[block], off_recv_sem.at[block]).wait()
        move = pltpu.make_async_copy(off_recv.at[block], off_smem.at[block], off_local_sem.at[block])
        move.start()
        move.wait()

    lane = lax.broadcasted_iota(jnp.int32, (2 * BINS, LANES), 1)
    inside = (chain != chains - 1).astype(jnp.float32)

    def res_copy(block, g):
        return pltpu.make_async_remote_copy(
            src_ref=res_send.at[block, g], dst_ref=res_recv.at[z],
            send_sem=res_send_sem.at[block, g], recv_sem=res_recv_sem.at[z],
            device_id=on_line(core * SEGS + g, block), device_id_type=MESH)

    def res_is_remote(block, g):
        return jnp.logical_or(core * SEGS + g != z, block != core)

    for phase in range(PHASES):
        def forward(s, _):
            white_wait(phase, 0, s)
            rim_copy(phase, s).start()
            for tile in range(2):
                wide[tile, s] = recv[phase, tile, s].astype(jnp.float32)
            return 0

        lax.fori_loop(0, SEGS, forward, 0)

        def take(s, _):
            white_wait(phase, 1, s)
            for tile in range(2, 4):
                wide[tile, s] = recv[phase, tile, s].astype(jnp.float32)
            return 0

        lax.fori_loop(0, SEGS, take, 0)

        def take_rim(s, _):
            rim_copy(phase, s).wait_recv()
            for tile in range(2):
                wide[4 + tile, s] = rim[phase, tile, s].astype(jnp.float32) * inside
            return 0

        lax.fori_loop(0, SEGS, take_rim, 0)

        for block in range(2):
            def slots(g, _):
                for j in range(2):
                    off = jnp.clip(off_smem[block, 0, 2 * g + j], 1, C)
                    skip = (off - 1) // LANES
                    rest = off - skip * LANES
                    first = lane < LANES - rest

                    def one_segment(s, acc):
                        tiles = [pltpu.roll(wide[2 * block + skip + i, s], LANES - rest, 1) for i in range(3)]
                        out = []
                        for tile in range(2):
                            own = wide[2 * block + tile, s]
                            own_re, own_im = own[:2 * BINS], own[2 * BINS:]
                            far_re = jnp.where(first, tiles[tile][:2 * BINS], tiles[tile + 1][:2 * BINS])
                            far_im = jnp.where(first, tiles[tile][2 * BINS:], tiles[tile + 1][2 * BINS:])
                            out.append(acc[2 * tile] + (own_re * far_re + own_im * far_im))
                            out.append(acc[2 * tile + 1] + (own_im * far_re - own_re * far_im))
                        return tuple(out)

                    zero = jnp.zeros((2 * BINS, LANES), jnp.float32)
                    acc = lax.fori_loop(0, SEGS, one_segment, (zero,) * 4, unroll=True)
                    for tile in range(2):
                        parts = [a[:BINS] + a[BINS:] for a in acc[2 * tile:2 * tile + 2]]
                        both = jnp.concatenate(parts, axis=0)
                        if phase > 0:
                            both = both + totals[block, 2 * g + j, tile]
                        if phase < PHASES - 1:
                            totals[block, 2 * g + j, tile] = both
                        else:
                            res_send[block, g, j * 2 * BINS:(j + 1) * 2 * BINS,
                                     tile * LANES:(tile + 1) * LANES] = both.astype(jnp.bfloat16)
                if phase == PHASES - 1:
                    @pl.when(res_is_remote(block, g))
                    def _():
                        res_copy(block, g).start()

                    @pl.when(jnp.logical_not(res_is_remote(block, g)))
                    def _():
                        pltpu.make_async_copy(res_send.at[block, g], res_recv.at[z], res_recv_sem.at[z]).start()
                return 0

            lax.fori_loop(0, SEGS, slots, 0)

    def finish(chip, _):
        pltpu.make_async_copy(res_send.at[0, 0], res_recv.at[chip], res_recv_sem.at[chip]).wait()
        return 0

    lax.fori_loop(0, CHIPS, finish, 0)
    for j in range(2):
        sums = res_recv[:, j * 2 * BINS:(j + 1) * 2 * BINS, :].reshape(2 * NF, C)
        out_ref[j] = lax.dot_general(sums, lag_ref[...], (((0,), (0,)), ((), ())),
                                     preferred_element_type=jnp.float32).astype(jnp.bfloat16)

    def drain(t, _):
        for phase in range(PHASES):
            @pl.when(jnp.logical_or(t != z, zh != core))
            def _():
                white_copy(phase, t).wait_send()
        return 0

    lax.fori_loop(0, CHIPS, drain, 0)

    def drain_more(s, _):
        for phase in range(PHASES):
            rim_copy(phase, s).wait_send()
        for block in range(2):
            @pl.when(res_is_remote(block, s))
            def _():
                res_copy(block, s).wait_send()
        return 0

    lax.fori_loop(0, SEGS, drain_more, 0)
    for half in range(2):
        @pl.when(off_is_remote(half))
        def _():
            off_copy(half).wait_send()


def shards(columns, records, alive, offsets):
    vmem = pl.BlockSpec(memory_space=pltpu.VMEM)
    rec = jnp.transpose(records[0], (1, 0, 2))
    call = pl.pallas_call(
        functools.partial(kernel, columns),
        out_shape=jax.ShapeDtypeStruct((2, C, NL), jnp.bfloat16),
        in_specs=[vmem] * 5,
        out_specs=vmem,
        scratch_shapes=[
            pltpu.VMEM((PHASES, CHIPS, 2, 4 * BINS, LANES), jnp.bfloat16),
            pltpu.VMEM((PHASES, 4, SEGS, 4 * BINS, LANES), jnp.bfloat16),
            pltpu.VMEM((PHASES, 2, SEGS, 4 * BINS, LANES), jnp.bfloat16),
            pltpu.VMEM((6, SEGS, 4 * BINS, LANES), jnp.float32),
            pltpu.VMEM((2, K, 2, 2 * BINS, LANES), jnp.float32),
            pltpu.VMEM((2, SEGS, 4 * BINS, C), jnp.bfloat16),
            pltpu.VMEM((CHIPS, 4 * BINS, C), jnp.bfloat16),
            pltpu.VMEM((8, LANES), jnp.int32),
            pltpu.VMEM((2, 8, LANES), jnp.int32),
            pltpu.SMEM((2, 8, LANES), jnp.int32),
            pltpu.SemaphoreType.DMA((PHASES, CHIPS)),
            pltpu.SemaphoreType.DMA((PHASES, 2, SEGS)),
            pltpu.SemaphoreType.DMA((PHASES, SEGS)),
            pltpu.SemaphoreType.DMA((PHASES, SEGS)),
            pltpu.SemaphoreType.DMA((2, SEGS)),
            pltpu.SemaphoreType.DMA((CHIPS,)),
            pltpu.SemaphoreType.DMA((2,)),
            pltpu.SemaphoreType.DMA((2,)),
            pltpu.SemaphoreType.DMA((2,)),
        ],
        compiler_params=pltpu.CompilerParams(
            collective_id=0, has_side_effects=True, vmem_limit_bytes=32 * 1024 * 1024),
        cost_estimate=pl.CostEstimate(flops=400_000_000, bytes_accessed=3_000_000, transcendentals=1024),
        name="line_correlate",
    )
    return call(rec, alive.reshape(1, C), offsets, forward_table(), lag_table().astype(jnp.bfloat16))


def solution(mesh):
    in_specs = (P("seg", "chan", None, None), P("chan"), P("chan", None))
    out_specs = P("seg", "chan", None)
    body = functools.partial(shards, mesh.shape["chan"] // 4)
    return jax.shard_map(body, mesh=mesh, in_specs=in_specs, out_specs=out_specs, check_vma=False)
```

time: 329 us -> 62.1 us (0.19); the launches traced: 324 us -> 61.9 us
  waiting for transfers between devices: 183 us -> 0 us
  Pallas kernels: 0 us -> 59 us
  loops' own time: 58.7 us -> 0 us
  other arithmetic: 30.8 us -> 0 us
  local copies, waits for them, and re-layouts: 23.9 us -> 2.83 us
  between operations: 13.6 us -> 0.05 us
  starting transfers between devices: 10.7 us -> 0 us
    psum x1 -> x0, waiting for transfers between devices: 170 us -> none  [shards(): total = lax.psum(terms.astype(jnp.bfloat16), 'seg').astype(jnp.float32)]
    pallas_call x0 -> x1, Pallas kernels: none -> 59 us  [shards(): call(rec, alive.reshape(1, C), offsets, forward_table(), lag_table().asty...]
    another operation x1 -> x0, loops' own time: 58.7 us -> none  [shards(): terms = lax.map(one_slot, jnp.arange(K, dtype=jnp.int32))]
    dynamic_slice x32 -> x0, local copies, waits for them, and re-layouts: 19.7 us -> none  [the longest x16 9.86 us: one_slot(): start = offsets[0, slot]]
    ppermute x2 -> x0, waiting for transfers between devices: 13.1 us -> none  [shifted(): return lax.ppermute(shard, axis, pairs)]
    reduce_sum x16 -> x0, other arithmetic: 12.2 us -> none  [pair_product(): real_part = jnp.sum(first_re * second_re + first_im * second_im, axis=1)]
    dynamic_update_slice x16 -> x0, other arithmetic: 10.8 us -> none  [shards(): terms = lax.map(one_slot, jnp.arange(K, dtype=jnp.int32))]
    ppermute x2 -> x0, starting transfers between devices: 10.7 us -> none  [shifted(): return lax.ppermute(shard, axis, pairs)]
  transfers between devices with their start and end apart: 3 -> 0, of which waited for: 2 -> 0; matrix products, arithmetic and copies ran while one was open for 2% -> 0% of each run, Pallas kernels for 0% -> 0%
where the time goes in v1:
time: 62.1 us; the launch traced here: 61.9 us
  Pallas kernels  59 us (95%)
  local copies, waits for them, and re-layouts  2.83 us (5%)
    pallas_call x1, Pallas kernels, shards(): call(rec, alive.reshape(1, C), offsets, forward_table(), lag_table().asty...  59 us
    unnamed x10, local copies, waits for them, and re-layouts  2.83 us

profile of v1, /device:TPU:1, one launch (start us, length us, event | category | flops | bytes accessed | tf_op | source)
XLA Modules:
  0.0 61.9 jit_solution(9835701370376494439)
XLA Ops:
  0.0 0.0 copy-start
  0.0 0.0 copy-start.1
  0.0 1.5 %copy.8 = bf16[1,256,4,512]{3,1,2,0:T(8,128)(2,1)S(1)} copy(bf16[1,256,4,512]{3,2,1,0:T(4,128)(2,1)} %param.5) | data formatting | bytes 2097152 | tf_op args[0]
  1.5 0.0 copy-start.2
  1.5 0.0 copy-start.3
  1.5 0.0 copy-done
  1.5 0.0 copy-done.1
  1.5 0.6 %copy-done.2 = s32[256]{0:T(256)S(1)} copy-done((s32[256]{0:T(256)S(1)}, s32[256]{0:T(256)}, u32[]{:S(2)}) %copy-start.2) | copy-done | bytes 1048
  2.2 0.0 copy-done.3
  2.2 59.0 %line_correlate.1 = bf16[2,256,256]{2,1,0:T(8,128)(2,1)S(1)} custom-call(bf16[4,256,512]{2,1,0:T(8,128)(2,1)S(1)} %bitcast.6, s32[1,256]{1,0:T(1,128)S(1)} %bitcast.7, s32[1,16]{1,0:T(1,128)S(1)} %copy-done.3, bf16[256,512]{1,0:T(8,128)(2,1)S(1)} %copy-done, bf16[256,256]{1,0:T(8,128)(2,1)S(1)} %copy-done.1), custom_call_target="tpu_custom_call" | custom-call | flops 400000000 | bytes 3000000 | tf_op jit(solution)/shard_map/line_correlate/pallas_call | solution.py:318
  61.2 0.7 %copy.10 = bf16[2,256,256]{2,1,0:T(8,128)(2,1)} copy(bf16[2,256,256]{2,1,0:T(8,128)(2,1)S(1)} %line_correlate.1) | data formatting | bytes 524288
Async XLA Ops:
  0.0 1.5 %copy-start = (bf16[256,512]{1,0:T(8,128)(2,1)S(1)}, bf16[256,512]{1,0:T(8,128)(2,1)}, u32[]{:S(2)}) copy-start(bf16[256,512]{1,0:T(8,128)(2,1)} %constant.8.tab_ref) | copy-start | bytes 786436
  0.0 1.5 %copy-start.1 = (bf16[256,256]{1,0:T(8,128)(2,1)S(1)}, bf16[256,256]{1,0:T(8,128)(2,1)}, u32[]{:S(2)}) copy-start(bf16[256,256]{1,0:T(8,128)(2,1)} %constant.9.lag_ref) | copy-start | bytes 393220
  1.5 0.7 %copy-start.2 = (s32[256]{0:T(256)S(1)}, s32[256]{0:T(256)}, u32[]{:S(2)}) copy-start(s32[256]{0:T(256)} %param.6) | copy-start | bytes 3076
  1.5 0.7 %copy-start.3 = (s32[1,16]{1,0:T(1,128)S(1)}, s32[1,16]{1,0:T(1,128)}, u32[]{:S(2)}) copy-start(s32[1,16]{1,0:T(1,128)} %off_ref.1) | copy-start | bytes 196

commit v2 on v1

v2 whole, which is shorter than its diff:
```python
import functools

import jax
import jax.numpy as jnp
import numpy as np
from jax import lax
from jax.experimental import pallas as pl
from jax.experimental.pallas import tpu as pltpu
from jax.sharding import PartitionSpec as P

W = 4
WIN = 512
NF = 128
F0 = 1
NL = 256
K = 16
C = 256
SEGS = 8
CHIPS = 16
PHASES = 2
BINS = NF // CHIPS // PHASES
ROWS = W * BINS
LANES = 128
GROUP = 8
STEP = 32
eps = 1e-06
MESH = pl.DeviceIdType.MESH
BOTH_MINOR = (((1,), (1,)), ((), ()))


def bin_order():
    phase, chip, part, which = np.meshgrid(
        np.arange(PHASES), np.arange(CHIPS), np.arange(2), np.arange(BINS), indexing="ij")
    return (F0 + (chip * PHASES + phase) * BINS + which).reshape(-1), part.reshape(-1)


def forward_table():
    bins, part = bin_order()
    turn = (bins[:, None] * np.arange(WIN)[None, :]) % WIN
    angle = turn * (2.0 * np.pi / WIN)
    rows = np.where(part[:, None] == 0, np.cos(angle), -np.sin(angle))
    return jnp.asarray(rows.astype(np.float32)).astype(jnp.bfloat16)


def lag_table():
    bins, part = bin_order()
    turn = (bins[:, None] * (np.arange(NL)[None, :] - NL // 2)) % WIN
    angle = turn * (2.0 * np.pi / WIN)
    rows = np.where(part[:, None] == 0, np.cos(angle), -np.sin(angle)) / NF
    return jnp.asarray(rows.astype(np.float32)).astype(jnp.bfloat16)


def identity():
    row = lax.broadcasted_iota(jnp.int32, (C, C), 0)
    column = lax.broadcasted_iota(jnp.int32, (C, C), 1)
    return (row == column).astype(jnp.float32).astype(jnp.bfloat16)


def selector():
    row = lax.broadcasted_iota(jnp.int32, (2 * BINS, 2 * LANES), 0)
    lane = lax.broadcasted_iota(jnp.int32, (2 * BINS, 2 * LANES), 1)
    same = jnp.logical_and(row % BINS == lane % BINS, row // BINS == lane // LANES)
    return same.astype(jnp.float32).astype(jnp.bfloat16)


def kernel(columns, rec_ref, alive_ref, off_ref, tab_ref, lag_ref, out_ref,
           raw, send, recv, rim, far, own, prod, res_send, res_recv, off_src, off_recv, off_smem,
           send_sem, recv_sem, rim_send_sem, rim_recv_sem, res_send_sem, res_recv_sem,
           off_send_sem, off_recv_sem, off_local_sem):
    chan = lax.axis_index("chan")
    seg = lax.axis_index("seg")
    core = chan % 2
    zh = (chan // 2) % 2
    col = chan // 4
    z = zh * SEGS + seg
    chain = col * 2 + core
    chains = columns * 2
    before = (chain + chains - 1) % chains
    after = (chain + 1) % chains

    def on_line(chip, which):
        return ((col * 2 + chip // SEGS) * 2 + which, chip % SEGS)

    def on_chain(link):
        return (((link // 2) * 2 + zh) * 2 + link % 2, seg)

    barrier = pltpu.get_barrier_semaphore()

    def greet(t, _):
        chip = (z + t) % CHIPS

        @pl.when(jnp.logical_or(chip != z, zh != core))
        def _():
            pl.semaphore_signal(barrier, 1, device_id=on_line(chip, zh), device_id_type=MESH)
        which = t % 2
        other = core * SEGS + t // 2

        @pl.when(jnp.logical_or(other != z, which != core))
        def _():
            pl.semaphore_signal(barrier, 1, device_id=on_line(other, which), device_id_type=MESH)
        return 0

    lax.fori_loop(0, 2 * SEGS, greet, 0)
    for link in (before, after):
        pl.semaphore_signal(barrier, 1, device_id=on_chain(link), device_id_type=MESH)

    off_src[...] = jnp.zeros_like(off_src)
    off_src[0:1, 0:K] = off_ref[...]
    live = alive_ref[...].astype(jnp.float32)

    def white_copy(phase, chip):
        return pltpu.make_async_remote_copy(
            src_ref=send.at[phase, chip], dst_ref=recv.at[phase, core, :, seg],
            send_sem=send_sem.at[phase, chip], recv_sem=recv_sem.at[phase, core, seg],
            device_id=on_line(chip, zh), device_id_type=MESH)

    def white_local(phase):
        return pltpu.make_async_copy(
            send.at[phase, z], recv.at[phase, core, :, seg], recv_sem.at[phase, core, seg])

    def white_wait(phase, block, s):
        pltpu.make_async_copy(
            send.at[phase, 0], recv.at[phase, block, :, s], recv_sem.at[phase, block, s]).wait()

    def rim_copy(phase, s):
        return pltpu.make_async_remote_copy(
            src_ref=recv.at[phase, 0, :, s], dst_ref=rim.at[phase, :, s],
            send_sem=rim_send_sem.at[phase, s], recv_sem=rim_recv_sem.at[phase, s],
            device_id=on_chain(before), device_id_type=MESH)

    def off_copy(half):
        return pltpu.make_async_remote_copy(
            src_ref=off_src, dst_ref=off_recv.at[core],
            send_sem=off_send_sem.at[half], recv_sem=off_recv_sem.at[core],
            device_id=on_line(half * SEGS + seg, zh), device_id_type=MESH)

    def off_is_remote(half):
        return jnp.logical_or(half != zh, zh != core)

    scales = []
    for w in range(W):
        spectra = lax.dot_general(tab_ref[...], rec_ref[w], BOTH_MINOR, preferred_element_type=jnp.float32)
        power = jnp.sum(spectra * spectra, axis=0, keepdims=True) * (1.0 / (2 * NF))
        scales.append((lax.rsqrt(power + eps) * live).reshape(1, 1, C))
        raw[w] = spectra.reshape(PHASES * CHIPS, 2 * BINS, C)
    upper = lax.broadcasted_iota(jnp.int32, (1, 2 * BINS, C), 1) < BINS
    some = 4
    for phase in range(PHASES):
        for first in range(0, CHIPS, some):
            real, imag = [], []
            for w in range(0, W, 2):
                at = slice(phase * CHIPS + first, phase * CHIPS + first + some)
                one, two = raw[w, at] * scales[w], raw[w + 1, at] * scales[w + 1]
                real.append(jnp.where(upper, one, pltpu.roll(two, BINS, 1)))
                imag.append(jnp.where(upper, pltpu.roll(one, BINS, 1), two))
            for part, rows in enumerate((real, imag)):
                send[phase, first:first + some, part] = jnp.concatenate(rows, axis=1).astype(jnp.bfloat16)

    met = 4 * SEGS + 2 - 2 * (zh == core).astype(jnp.int32)
    pl.semaphore_wait(barrier, met)
    for half in range(2):
        @pl.when(off_is_remote(half))
        def _():
            off_copy(half).start()

        @pl.when(jnp.logical_not(off_is_remote(half)))
        def _():
            pltpu.make_async_copy(off_src, off_recv.at[core], off_recv_sem.at[core]).start()

    def chip_of(t):
        turn = CHIPS - 1 - t
        away = jnp.where(turn % 2 == 1, (turn + 1) // 2, CHIPS - turn // 2)
        return (z + away) % CHIPS

    def send_white(phase, t):
        chip = chip_of(t)
        remote = jnp.logical_or(chip != z, zh != core)

        @pl.when(remote)
        def _():
            if phase > 0:
                white_copy(phase - 1, chip).wait_send()
            white_copy(phase, chip).start()

        @pl.when(jnp.logical_not(remote))
        def _():
            white_local(phase).start()

    for phase in range(PHASES):
        def send_one(t, _):
            send_white(phase, t)
            return 0

        lax.fori_loop(0, CHIPS, send_one, 0)

    for block in range(2):
        pltpu.make_async_copy(off_src, off_recv.at[block], off_recv_sem.at[block]).wait()
        move = pltpu.make_async_copy(off_recv.at[block], off_smem.at[block], off_local_sem.at[block])
        move.start()
        move.wait()

    inside = (chain != chains - 1).astype(jnp.float32)
    turned = identity()
    summed = selector()

    def res_copy(phase, block, g):
        return pltpu.make_async_remote_copy(
            src_ref=res_send.at[phase, block, g], dst_ref=res_recv.at[phase, z],
            send_sem=res_send_sem.at[phase, block, g], recv_sem=res_recv_sem.at[phase, z],
            device_id=on_line(core * SEGS + g, block), device_id_type=MESH)

    def res_is_remote(block, g):
        return jnp.logical_or(core * SEGS + g != z, block != core)

    def transposed(rows):
        return lax.dot_general(turned, rows.reshape(SEGS * ROWS, C), BOTH_MINOR, preferred_element_type=jnp.float32)

    for phase in range(PHASES):
        for block in range(2):
            def arrive(s, _):
                white_wait(phase, block, s)
                if block == 0:
                    rim_copy(phase, s).start()
                return 0

            lax.fori_loop(0, SEGS, arrive, 0)
            for part in range(2):
                flipped = transposed(recv[phase, block, part])
                far[part, block * C:(block + 1) * C] = flipped
                own[part, block * C:(block + 1) * C] = flipped.astype(jnp.bfloat16)

        for block in range(2):
            if block == 1:
                def take_rim(s, _):
                    rim_copy(phase, s).wait_recv()
                    return 0

                lax.fori_loop(0, SEGS, take_rim, 0)
                for part in range(2):
                    far[part, 2 * C:3 * C] = transposed(rim[phase, part]) * inside

            def slots(group, _):
                offs = [jnp.clip(off_smem[block, 0, GROUP * group + j], 1, C) for j in range(GROUP)]
                for low in range(0, C, STEP):
                    own_re = own[0, block * C + low:block * C + low + STEP]
                    own_im = own[1, block * C + low:block * C + low + STEP]
                    for j in range(GROUP):
                        rows = pl.ds(block * C + low + offs[j], STEP)
                        far_re = far[0, rows, :].astype(jnp.bfloat16)
                        far_im = far[1, rows, :].astype(jnp.bfloat16)
                        prod[j * C + low:j * C + low + STEP, 0:LANES] = own_re * far_re + own_im * far_im
                        prod[j * C + low:j * C + low + STEP, LANES:2 * LANES] = own_im * far_re - own_re * far_im
                sums = lax.dot_general(summed, prod[...], BOTH_MINOR, preferred_element_type=jnp.float32)
                for i in range(GROUP // 2):
                    g = group * (GROUP // 2) + i
                    pair = [sums[:, (2 * i + j) * C:(2 * i + j + 1) * C] for j in range(2)]
                    res_send[phase, block, g] = jnp.concatenate(pair, axis=0).astype(jnp.bfloat16)

                    @pl.when(res_is_remote(block, g))
                    def _():
                        res_copy(phase, block, g).start()

                    @pl.when(jnp.logical_not(res_is_remote(block, g)))
                    def _():
                        pltpu.make_async_copy(
                            res_send.at[phase, block, g], res_recv.at[phase, z], res_recv_sem.at[phase, z]).start()
                return 0

            lax.fori_loop(0, K // GROUP, slots, 0)

    def finish(chip, _):
        for phase in range(PHASES):
            pltpu.make_async_copy(
                res_send.at[phase, 0, 0], res_recv.at[phase, chip], res_recv_sem.at[phase, chip]).wait()
        return 0

    lax.fori_loop(0, CHIPS, finish, 0)
    whole = res_recv[...].astype(jnp.float32).reshape(PHASES * CHIPS, 2, 2 * BINS, C)
    for j in range(2):
        sums = whole[:, j].reshape(2 * NF, C).astype(jnp.bfloat16)
        out_ref[j] = lax.dot_general(sums, lag_ref[...], (((0,), (0,)), ((), ())),
                                     preferred_element_type=jnp.float32).astype(jnp.bfloat16)

    def drain(t, _):
        @pl.when(jnp.logical_or(t != z, zh != core))
        def _():
            white_copy(PHASES - 1, t).wait_send()
        return 0

    lax.fori_loop(0, CHIPS, drain, 0)

    def drain_more(s, _):
        for phase in range(PHASES):
            rim_copy(phase, s).wait_send()
            for block in range(2):
                @pl.when(res_is_remote(block, s))
                def _():
                    res_copy(phase, block, s).wait_send()
        return 0

    lax.fori_loop(0, SEGS, drain_more, 0)
    for half in range(2):
        @pl.when(off_is_remote(half))
        def _():
            off_copy(half).wait_send()


def shards(columns, records, alive, offsets):
    vmem = pl.BlockSpec(memory_space=pltpu.VMEM)
    rec = jnp.transpose(records[0], (1, 0, 2))
    dma = pltpu.SemaphoreType.DMA
    call = pl.pallas_call(
        functools.partial(kernel, columns),
        out_shape=jax.ShapeDtypeStruct((2, C, NL), jnp.bfloat16),
        in_specs=[vmem] * 5,
        out_specs=vmem,
        scratch_shapes=[
            pltpu.VMEM((W, PHASES * CHIPS, 2 * BINS, C), jnp.float32),
            pltpu.VMEM((PHASES, CHIPS, 2, ROWS, C), jnp.bfloat16),
            pltpu.VMEM((PHASES, 2, 2, SEGS, ROWS, C), jnp.bfloat16),
            pltpu.VMEM((PHASES, 2, SEGS, ROWS, C), jnp.bfloat16),
            pltpu.VMEM((2, 3 * C, LANES), jnp.float32),
            pltpu.VMEM((2, 2 * C, LANES), jnp.bfloat16),
            pltpu.VMEM((GROUP * C, 2 * LANES), jnp.bfloat16),
            pltpu.VMEM((PHASES, 2, SEGS, 4 * BINS, C), jnp.bfloat16),
            pltpu.VMEM((PHASES, CHIPS, 4 * BINS, C), jnp.bfloat16),
            pltpu.VMEM((8, LANES), jnp.int32),
            pltpu.VMEM((2, 8, LANES), jnp.int32),
            pltpu.SMEM((2, 8, LANES), jnp.int32),
            dma((PHASES, CHIPS)),
            dma((PHASES, 2, SEGS)),
            dma((PHASES, SEGS)),
            dma((PHASES, SEGS)),
            dma((PHASES, 2, SEGS)),
            dma((PHASES, CHIPS)),
            dma((2,)),
            dma((2,)),
            dma((2,)),
        ],
        compiler_params=pltpu.CompilerParams(
            collective_id=0, has_side_effects=True, vmem_limit_bytes=32 * 1024 * 1024),
        cost_estimate=pl.CostEstimate(flops=400_000_000, bytes_accessed=3_000_000, transcendentals=1024),
        name="line_correlate",
    )
    return call(rec, alive.reshape(1, C), offsets, forward_table(), lag_table())


def solution(mesh):
    in_specs = (P("seg", "chan", None, None), P("chan"), P("chan", None))
    out_specs = P("seg", "chan", None)
    body = functools.partial(shards, mesh.shape["chan"] // 4)
    return jax.shard_map(body, mesh=mesh, in_specs=in_specs, out_specs=out_specs, check_vma=False)
```

time: 62.1 us -> 58.3 us (0.939); the launches traced: 61.9 us -> 57.2 us
  Pallas kernels: 59 us -> 54.3 us
    pallas_call x1, Pallas kernels: 59 us -> 54.3 us  [shards(): return call(rec, alive.reshape(1, C), offsets, forward_table(), lag_table())]
where the time goes in v2:
time: 58.3 us; the launch traced here: 57.2 us
  Pallas kernels  54.3 us (93%)
  local copies, waits for them, and re-layouts  2.83 us (5%)
    pallas_call x1, Pallas kernels, shards(): return call(rec, alive.reshape(1, C), offsets, forward_table(), lag_table())  54.3 us
    unnamed x10, local copies, waits for them, and re-layouts  2.83 us

profile of v2, /device:TPU:1, one launch (start us, length us, event | category | flops | bytes accessed | tf_op | source)
XLA Modules:
  0.0 57.2 jit_solution(9827764181685073003)
XLA Ops:
  0.0 0.0 copy-start
  0.0 0.0 copy-start.1
  0.0 1.5 %copy.8 = bf16[1,256,4,512]{3,1,2,0:T(8,128)(2,1)S(1)} copy(bf16[1,256,4,512]{3,2,1,0:T(4,128)(2,1)} %param.5) | data formatting | bytes 2097152 | tf_op args[0]
  1.5 0.0 copy-start.2
  1.5 0.0 copy-start.3
  1.5 0.0 copy-done
  1.5 0.0 copy-done.1
  1.5 0.6 %copy-done.2 = s32[256]{0:T(256)S(1)} copy-done((s32[256]{0:T(256)S(1)}, s32[256]{0:T(256)}, u32[]{:S(2)}) %copy-start.2) | copy-done | bytes 1048
  2.2 0.0 copy-done.3
  2.2 54.3 %line_correlate.1 = bf16[2,256,256]{2,1,0:T(8,128)(2,1)S(1)} custom-call(bf16[4,256,512]{2,1,0:T(8,128)(2,1)S(1)} %bitcast.6, s32[1,256]{1,0:T(1,128)S(1)} %bitcast.7, s32[1,16]{1,0:T(1,128)S(1)} %copy-done.3, bf16[256,512]{1,0:T(8,128)(2,1)S(1)} %copy-done, bf16[256,256]{1,0:T(8,128)(2,1)S(1)} %copy-done.1), custom_call_target="tpu_custom_call" | custom-call | flops 400000000 | bytes 3000000 | tf_op jit(solution)/shard_map/line_correlate/pallas_call | solution.py:345
  56.5 0.7 %copy.10 = bf16[2,256,256]{2,1,0:T(8,128)(2,1)} copy(bf16[2,256,256]{2,1,0:T(8,128)(2,1)S(1)} %line_correlate.1) | data formatting | bytes 524288
Async XLA Ops:
  0.0 1.5 %copy-start = (bf16[256,512]{1,0:T(8,128)(2,1)S(1)}, bf16[256,512]{1,0:T(8,128)(2,1)}, u32[]{:S(2)}) copy-start(bf16[256,512]{1,0:T(8,128)(2,1)} %constant.8.tab_ref) | copy-start | bytes 786436
  0.0 1.5 %copy-start.1 = (bf16[256,256]{1,0:T(8,128)(2,1)S(1)}, bf16[256,256]{1,0:T(8,128)(2,1)}, u32[]{:S(2)}) copy-start(bf16[256,256]{1,0:T(8,128)(2,1)} %constant.9.lag_ref) | copy-start | bytes 393220
  1.5 0.7 %copy-start.2 = (s32[256]{0:T(256)S(1)}, s32[256]{0:T(256)}, u32[]{:S(2)}) copy-start(s32[256]{0:T(256)} %param.6) | copy-start | bytes 3076
  1.5 0.7 %copy-start.3 = (s32[1,16]{1,0:T(1,128)S(1)}, s32[1,16]{1,0:T(1,128)}, u32[]{:S(2)}) copy-start(s32[1,16]{1,0:T(1,128)} %off_ref.1) | copy-start | bytes 196

commit v3 on v2

--- a/solution.py
+++ b/solution.py
@@ -39,7 +39,7 @@
     turn = (bins[:, None] * np.arange(WIN)[None, :]) % WIN
     angle = turn * (2.0 * np.pi / WIN)
     rows = np.where(part[:, None] == 0, np.cos(angle), -np.sin(angle))
-    return jnp.asarray(rows.astype(np.float32)).astype(jnp.bfloat16)
+    return jnp.asarray(rows.astype(np.float32))
 
 
 def lag_table():
@@ -47,7 +47,7 @@
     turn = (bins[:, None] * (np.arange(NL)[None, :] - NL // 2)) % WIN
     angle = turn * (2.0 * np.pi / WIN)
     rows = np.where(part[:, None] == 0, np.cos(angle), -np.sin(angle)) / NF
-    return jnp.asarray(rows.astype(np.float32)).astype(jnp.bfloat16)
+    return jnp.asarray(rows.astype(np.float32))
 
 
 def identity():
@@ -63,10 +63,10 @@
     return same.astype(jnp.float32).astype(jnp.bfloat16)
 
 
-def kernel(columns, rec_ref, alive_ref, off_ref, tab_ref, lag_ref, out_ref,
-           raw, send, recv, rim, far, own, prod, res_send, res_recv, off_src, off_recv, off_smem,
+def kernel(columns, rec_hbm, alive_hbm, off_hbm, tab_hbm, lag_hbm, out_ref,
+           rec_ref, alive_ref, off_ref, tab_ref, lag_ref, raw, send, recv, rim, far, own, prod, res_send, res_recv, off_src, off_recv, off_smem,
            send_sem, recv_sem, rim_send_sem, rim_recv_sem, res_send_sem, res_recv_sem,
-           off_send_sem, off_recv_sem, off_local_sem):
+           off_send_sem, off_recv_sem, off_local_sem, load_sem):
     chan = lax.axis_index("chan")
     seg = lax.axis_index("seg")
     core = chan % 2
@@ -87,11 +87,6 @@
     barrier = pltpu.get_barrier_semaphore()
 
     def greet(t, _):
-        chip = (z + t) % CHIPS
-
-        @pl.when(jnp.logical_or(chip != z, zh != core))
-        def _():
-            pl.semaphore_signal(barrier, 1, device_id=on_line(chip, zh), device_id_type=MESH)
         which = t % 2
         other = core * SEGS + t // 2
 
@@ -101,9 +96,14 @@
         return 0
 
     lax.fori_loop(0, 2 * SEGS, greet, 0)
-    for link in (before, after):
-        pl.semaphore_signal(barrier, 1, device_id=on_chain(link), device_id_type=MESH)
-
+    pl.semaphore_signal(barrier, 1, device_id=on_chain(after), device_id_type=MESH)
+
+    loads = [pltpu.make_async_copy(source, target, load_sem.at[i]) for i, (source, target) in enumerate((
+        (rec_hbm, rec_ref), (tab_hbm, tab_ref), (alive_hbm, alive_ref), (off_hbm, off_ref), (lag_hbm, lag_ref)))]
+    for load in loads:
+        load.start()
+    for load in loads:
+        load.wait()
     off_src[...] = jnp.zeros_like(off_src)
     off_src[0:1, 0:K] = off_ref[...]
     live = alive_ref[...].astype(jnp.float32)
@@ -137,9 +137,11 @@
     def off_is_remote(half):
         return jnp.logical_or(half != zh, zh != core)
 
+    table = tab_ref[...].astype(jnp.bfloat16)
+    by_window = jnp.swapaxes(rec_ref[0], 0, 1)
     scales = []
     for w in range(W):
-        spectra = lax.dot_general(tab_ref[...], rec_ref[w], BOTH_MINOR, preferred_element_type=jnp.float32)
+        spectra = lax.dot_general(table, by_window[w], BOTH_MINOR, preferred_element_type=jnp.float32)
         power = jnp.sum(spectra * spectra, axis=0, keepdims=True) * (1.0 / (2 * NF))
         scales.append((lax.rsqrt(power + eps) * live).reshape(1, 1, C))
         raw[w] = spectra.reshape(PHASES * CHIPS, 2 * BINS, C)
@@ -156,7 +158,7 @@
             for part, rows in enumerate((real, imag)):
                 send[phase, first:first + some, part] = jnp.concatenate(rows, axis=1).astype(jnp.bfloat16)
 
-    met = 4 * SEGS + 2 - 2 * (zh == core).astype(jnp.int32)
+    met = CHIPS + 1 - (zh == core).astype(jnp.int32)
     pl.semaphore_wait(barrier, met)
     for half in range(2):
         @pl.when(off_is_remote(half))
@@ -167,13 +169,12 @@
         def _():
             pltpu.make_async_copy(off_src, off_recv.at[core], off_recv_sem.at[core]).start()
 
-    def chip_of(t):
+    def away(t):
         turn = CHIPS - 1 - t
-        away = jnp.where(turn % 2 == 1, (turn + 1) // 2, CHIPS - turn // 2)
-        return (z + away) % CHIPS
+        return jnp.where(turn % 2 == 1, (turn + 1) // 2, CHIPS - turn // 2)
 
     def send_white(phase, t):
-        chip = chip_of(t)
+        chip = (z + away(t)) % CHIPS
         remote = jnp.logical_or(chip != z, zh != core)
 
         @pl.when(remote)
@@ -216,14 +217,19 @@
         return lax.dot_general(turned, rows.reshape(SEGS * ROWS, C), BOTH_MINOR, preferred_element_type=jnp.float32)
 
     for phase in range(PHASES):
+        def arrive(t, _):
+            chip = (z + CHIPS - away(t)) % CHIPS
+
+            @pl.when(chip // SEGS == core)
+            def _():
+                s = chip % SEGS
+                white_wait(phase, 0, s)
+                rim_copy(phase, s).start()
+                white_wait(phase, 1, s)
+            return 0
+
+        lax.fori_loop(0, CHIPS, arrive, 0)
         for block in range(2):
-            def arrive(s, _):
-                white_wait(phase, block, s)
-                if block == 0:
-                    rim_copy(phase, s).start()
-                return 0
-
-            lax.fori_loop(0, SEGS, arrive, 0)
             for part in range(2):
                 flipped = transposed(recv[phase, block, part])
                 far[part, block * C:(block + 1) * C] = flipped
@@ -268,18 +274,23 @@
 
             lax.fori_loop(0, K // GROUP, slots, 0)
 
-    def finish(chip, _):
-        for phase in range(PHASES):
+    lags = lag_ref[...].astype(jnp.bfloat16)
+    result = [0.0, 0.0]
+    for phase in range(PHASES):
+        def finish(chip, _):
             pltpu.make_async_copy(
                 res_send.at[phase, 0, 0], res_recv.at[phase, chip], res_recv_sem.at[phase, chip]).wait()
-        return 0
-
-    lax.fori_loop(0, CHIPS, finish, 0)
-    whole = res_recv[...].astype(jnp.float32).reshape(PHASES * CHIPS, 2, 2 * BINS, C)
+            return 0
+
+        lax.fori_loop(0, CHIPS, finish, 0)
+        whole = res_recv[phase].astype(jnp.float32).reshape(CHIPS, 2, 2 * BINS, C)
+        rows = slice(phase * CHIPS * 2 * BINS, (phase + 1) * CHIPS * 2 * BINS)
+        for j in range(2):
+            sums = whole[:, j].reshape(CHIPS * 2 * BINS, C).astype(jnp.bfloat16)
+            result[j] += lax.dot_general(sums, lags[rows], (((0,), (0,)), ((), ())),
+                                         preferred_element_type=jnp.float32)
     for j in range(2):
-        sums = whole[:, j].reshape(2 * NF, C).astype(jnp.bfloat16)
-        out_ref[j] = lax.dot_general(sums, lag_ref[...], (((0,), (0,)), ((), ())),
-                                     preferred_element_type=jnp.float32).astype(jnp.bfloat16)
+        out_ref[j] = result[j].astype(jnp.bfloat16)
 
     def drain(t, _):
         @pl.when(jnp.logical_or(t != z, zh != core))
@@ -307,14 +318,18 @@
 
 def shards(columns, records, alive, offsets):
     vmem = pl.BlockSpec(memory_space=pltpu.VMEM)
-    rec = jnp.transpose(records[0], (1, 0, 2))
     dma = pltpu.SemaphoreType.DMA
     call = pl.pallas_call(
         functools.partial(kernel, columns),
         out_shape=jax.ShapeDtypeStruct((2, C, NL), jnp.bfloat16),
-        in_specs=[vmem] * 5,
+        in_specs=[pl.BlockSpec(memory_space=pltpu.HBM)] * 5,
         out_specs=vmem,
         scratch_shapes=[
+            pltpu.VMEM((1, C, W, WIN), jnp.bfloat16),
+            pltpu.VMEM((1, C), jnp.int32),
+            pltpu.VMEM((1, K), jnp.int32),
+            pltpu.VMEM((2 * NF, WIN), jnp.float32),
+            pltpu.VMEM((2 * NF, NL), jnp.float32),
             pltpu.VMEM((W, PHASES * CHIPS, 2 * BINS, C), jnp.float32),
             pltpu.VMEM((PHASES, CHIPS, 2, ROWS, C), jnp.bfloat16),
             pltpu.VMEM((PHASES, 2, 2, SEGS, ROWS, C), jnp.bfloat16),
@@ -336,13 +351,14 @@
             dma((2,)),
             dma((2,)),
             dma((2,)),
+            dma((5,)),
         ],
         compiler_params=pltpu.CompilerParams(
-            collective_id=0, has_side_effects=True, vmem_limit_bytes=32 * 1024 * 1024),
+            collective_id=0, has_side_effects=True, vmem_limit_bytes=56 * 1024 * 1024),
         cost_estimate=pl.CostEstimate(flops=400_000_000, bytes_accessed=3_000_000, transcendentals=1024),
         name="line_correlate",
     )
-    return call(rec, alive.reshape(1, C), offsets, forward_table(), lag_table())
+    return call(records, alive.reshape(1, C), offsets, forward_table(), lag_table())
 
 
 def solution(mesh):

time: 58.3 us -> 57.5 us (0.986)
  local copies, waits for them, and re-layouts: 2.83 us -> 1.67 us
  Pallas kernels: 54.3 us -> 55 us
    unnamed x10 -> x1, local copies, waits for them, and re-layouts: 2.83 us -> 1.67 us
    pallas_call x1, Pallas kernels: 54.3 us -> 55 us  [shards(): call(records, alive.reshape(1, C), offsets, forward_table(), lag_table())]
where the time goes in v3:
time: 57.5 us; the launch traced here: 56.7 us
  Pallas kernels  55 us (96%)
  local copies, waits for them, and re-layouts  1.67 us (3%)
    pallas_call x1, Pallas kernels, shards(): call(records, alive.reshape(1, C), offsets, forward_table(), lag_table())  55 us
    unnamed x1, local copies, waits for them, and re-layouts  1.67 us

profile of v3, /device:TPU:1, one launch (start us, length us, event | category | flops | bytes accessed | tf_op | source)
XLA Modules:
  0.0 56.7 jit_solution(1625065416828284333)
XLA Ops:
  0.0 55.0 %line_correlate.1 = bf16[2,256,256]{2,1,0:T(8,128)(2,1)} custom-call(bf16[1,256,4,512]{3,2,1,0:T(4,128)(2,1)} %rec_hbm.1, s32[1,256]{1,0:T(1,128)} %bitcast.1, s32[1,16]{1,0:T(1,128)} %off_hbm.1, f32[256,512]{1,0:T(8,128)} %constant.4.clone.tab_hbm, f32[256,256]{1,0:T(8,128)} %constant.5.clone.lag_hbm), custom_call_target="tpu_custom_call" | custom-call | flops 400000000 | bytes 3000000 | tf_op jit(solution)/shard_map/line_correlate/pallas_call | solution.py:361
  55.0 1.7 %copy.7 = bf16[2,256,256]{2,1,0:T(8,128)(2,1)} copy(bf16[2,256,256]{2,1,0:T(8,128)(2,1)} %line_correlate.1) | data formatting | bytes 524288

commit v4 on v3

--- a/solution.py
+++ b/solution.py
@@ -34,20 +34,15 @@
     return (F0 + (chip * PHASES + phase) * BINS + which).reshape(-1), part.reshape(-1)
 
 
-def forward_table():
+def tables():
     bins, part = bin_order()
-    turn = (bins[:, None] * np.arange(WIN)[None, :]) % WIN
-    angle = turn * (2.0 * np.pi / WIN)
-    rows = np.where(part[:, None] == 0, np.cos(angle), -np.sin(angle))
-    return jnp.asarray(rows.astype(np.float32))
-
-
-def lag_table():
-    bins, part = bin_order()
-    turn = (bins[:, None] * (np.arange(NL)[None, :] - NL // 2)) % WIN
-    angle = turn * (2.0 * np.pi / WIN)
-    rows = np.where(part[:, None] == 0, np.cos(angle), -np.sin(angle)) / NF
-    return jnp.asarray(rows.astype(np.float32))
+
+    def rows(times):
+        angle = ((bins[:, None] * times[None, :]) % WIN) * (2.0 * np.pi / WIN)
+        return np.where(part[:, None] == 0, np.cos(angle), -np.sin(angle))
+
+    both = np.concatenate([rows(np.arange(WIN)), rows(np.arange(NL) - NL // 2) / NF], axis=1)
+    return jnp.asarray(both.astype(np.float32))
 
 
 def identity():
@@ -63,8 +58,8 @@
     return same.astype(jnp.float32).astype(jnp.bfloat16)
 
 
-def kernel(columns, rec_hbm, alive_hbm, off_hbm, tab_hbm, lag_hbm, out_ref,
-           rec_ref, alive_ref, off_ref, tab_ref, lag_ref, raw, send, recv, rim, far, own, prod, res_send, res_recv, off_src, off_recv, off_smem,
+def kernel(columns, rec_hbm, alive_hbm, off_hbm, tab_hbm, out_ref,
+           rec_ref, alive_ref, off_ref, tab_ref, raw, send, recv, rim, far, own, prod, res_send, res_recv, off_src, off_recv, off_smem,
            send_sem, recv_sem, rim_send_sem, rim_recv_sem, res_send_sem, res_recv_sem,
            off_send_sem, off_recv_sem, off_local_sem, load_sem):
     chan = lax.axis_index("chan")
@@ -86,20 +81,17 @@
 
     barrier = pltpu.get_barrier_semaphore()
 
-    def greet(t, _):
-        which = t % 2
-        other = core * SEGS + t // 2
-
-        @pl.when(jnp.logical_or(other != z, which != core))
-        def _():
-            pl.semaphore_signal(barrier, 1, device_id=on_line(other, which), device_id_type=MESH)
-        return 0
-
-    lax.fori_loop(0, 2 * SEGS, greet, 0)
+    for s in range(SEGS):
+        for which in range(2):
+            sender = ((col * 2 + core) * 2 + which, s)
+
+            @pl.when(jnp.logical_or(sender[0] != chan, s != seg))
+            def _():
+                pl.semaphore_signal(barrier, 1, device_id=sender, device_id_type=MESH)
     pl.semaphore_signal(barrier, 1, device_id=on_chain(after), device_id_type=MESH)
 
     loads = [pltpu.make_async_copy(source, target, load_sem.at[i]) for i, (source, target) in enumerate((
-        (rec_hbm, rec_ref), (tab_hbm, tab_ref), (alive_hbm, alive_ref), (off_hbm, off_ref), (lag_hbm, lag_ref)))]
+        (rec_hbm, rec_ref), (tab_hbm, tab_ref), (alive_hbm, alive_ref), (off_hbm, off_ref)))]
     for load in loads:
         load.start()
     for load in loads:
@@ -137,7 +129,7 @@
     def off_is_remote(half):
         return jnp.logical_or(half != zh, zh != core)
 
-    table = tab_ref[...].astype(jnp.bfloat16)
+    table = tab_ref[:, :WIN].astype(jnp.bfloat16)
     by_window = jnp.swapaxes(rec_ref[0], 0, 1)
     scales = []
     for w in range(W):
@@ -213,6 +205,18 @@
     def res_is_remote(block, g):
         return jnp.logical_or(core * SEGS + g != z, block != core)
 
+    def send_sums(phase, block, g):
+        remote = res_is_remote(block, g)
+
+        @pl.when(remote)
+        def _():
+            res_copy(phase, block, g).start()
+
+        @pl.when(jnp.logical_not(remote))
+        def _():
+            pltpu.make_async_copy(
+                res_send.at[phase, block, g], res_recv.at[phase, z], res_recv_sem.at[phase, z]).start()
+
     def transposed(rows):
         return lax.dot_general(turned, rows.reshape(SEGS * ROWS, C), BOTH_MINOR, preferred_element_type=jnp.float32)
 
@@ -235,8 +239,33 @@
                 far[part, block * C:(block + 1) * C] = flipped
                 own[part, block * C:(block + 1) * C] = flipped.astype(jnp.bfloat16)
 
-        for block in range(2):
-            if block == 1:
+        def one_group(block, group):
+            offs = [jnp.clip(off_smem[block, 0, GROUP * group + j], 1, C) for j in range(GROUP)]
+            for low in range(0, C, STEP):
+                own_re = own[0, block * C + low:block * C + low + STEP]
+                own_im = own[1, block * C + low:block * C + low + STEP]
+                for j in range(GROUP):
+                    rows = pl.ds(block * C + low + offs[j], STEP)
+                    far_re = far[0, rows, :].astype(jnp.bfloat16)
+                    far_im = far[1, rows, :].astype(jnp.bfloat16)
+                    prod[j * C + low:j * C + low + STEP, 0:LANES] = own_re * far_re + own_im * far_im
+                    prod[j * C + low:j * C + low + STEP, LANES:2 * LANES] = own_im * far_re - own_re * far_im
+            sums = lax.dot_general(summed, prod[...], BOTH_MINOR, preferred_element_type=jnp.float32)
+            for i in range(GROUP // 2):
+                g = group * (GROUP // 2) + i
+                pair = [sums[:, (2 * i + j) * C:(2 * i + j + 1) * C] for j in range(2)]
+                res_send[phase, block, g] = jnp.concatenate(pair, axis=0).astype(jnp.bfloat16)
+                send_sums(phase, block, g)
+
+        def both_blocks(group, _):
+            one_group(0, group)
+            if_rim(group)
+            one_group(1, group)
+            return 0
+
+        def if_rim(group):
+            @pl.when(group == 0)
+            def _():
                 def take_rim(s, _):
                     rim_copy(phase, s).wait_recv()
                     return 0
@@ -245,36 +274,8 @@
                 for part in range(2):
                     far[part, 2 * C:3 * C] = transposed(rim[phase, part]) * inside
 
-            def slots(group, _):
-                offs = [jnp.clip(off_smem[block, 0, GROUP * group + j], 1, C) for j in range(GROUP)]
-                for low in range(0, C, STEP):
-                    own_re = own[0, block * C + low:block * C + low + STEP]
-                    own_im = own[1, block * C + low:block * C + low + STEP]
-                    for j in range(GROUP):
-                        rows = pl.ds(block * C + low + offs[j], STEP)
-                        far_re = far[0, rows, :].astype(jnp.bfloat16)
-                        far_im = far[1, rows, :].astype(jnp.bfloat16)
-                        prod[j * C + low:j * C + low + STEP, 0:LANES] = own_re * far_re + own_im * far_im
-                        prod[j * C + low:j * C + low + STEP, LANES:2 * LANES] = own_im * far_re - own_re * far_im
-                sums = lax.dot_general(summed, prod[...], BOTH_MINOR, preferred_element_type=jnp.float32)
-                for i in range(GROUP // 2):
-                    g = group * (GROUP // 2) + i
-                    pair = [sums[:, (2 * i + j) * C:(2 * i + j + 1) * C] for j in range(2)]
-                    res_send[phase, block, g] = jnp.concatenate(pair, axis=0).astype(jnp.bfloat16)
-
-                    @pl.when(res_is_remote(block, g))
-                    def _():
-                        res_copy(phase, block, g).start()
-
-                    @pl.when(jnp.logical_not(res_is_remote(block, g)))
-                    def _():
-                        pltpu.make_async_copy(
-                            res_send.at[phase, block, g], res_recv.at[phase, z], res_recv_sem.at[phase, z]).start()
-                return 0
-
-            lax.fori_loop(0, K // GROUP, slots, 0)
-
-    lags = lag_ref[...].astype(jnp.bfloat16)
+        lax.fori_loop(0, K // GROUP, both_blocks, 0)
+    lags = tab_ref[:, WIN:].astype(jnp.bfloat16)
     result = [0.0, 0.0]
     for phase in range(PHASES):
         def finish(chip, _):
@@ -322,14 +323,13 @@
     call = pl.pallas_call(
         functools.partial(kernel, columns),
         out_shape=jax.ShapeDtypeStruct((2, C, NL), jnp.bfloat16),
-        in_specs=[pl.BlockSpec(memory_space=pltpu.HBM)] * 5,
+        in_specs=[pl.BlockSpec(memory_space=pltpu.HBM)] * 4,
         out_specs=vmem,
         scratch_shapes=[
             pltpu.VMEM((1, C, W, WIN), jnp.bfloat16),
             pltpu.VMEM((1, C), jnp.int32),
             pltpu.VMEM((1, K), jnp.int32),
-            pltpu.VMEM((2 * NF, WIN), jnp.float32),
-            pltpu.VMEM((2 * NF, NL), jnp.float32),
+            pltpu.VMEM((2 * NF, WIN + NL), jnp.float32),
             pltpu.VMEM((W, PHASES * CHIPS, 2 * BINS, C), jnp.float32),
             pltpu.VMEM((PHASES, CHIPS, 2, ROWS, C), jnp.bfloat16),
             pltpu.VMEM((PHASES, 2, 2, SEGS, ROWS, C), jnp.bfloat16),
@@ -351,14 +351,14 @@
             dma((2,)),
             dma((2,)),
             dma((2,)),
-            dma((5,)),
+            dma((4,)),
         ],
         compiler_params=pltpu.CompilerParams(
-            collective_id=0, has_side_effects=True, vmem_limit_bytes=56 * 1024 * 1024),
+            collective_id=0, has_side_effects=True, vmem_limit_bytes=53 * 1024 * 1024),
         cost_estimate=pl.CostEstimate(flops=400_000_000, bytes_accessed=3_000_000, transcendentals=1024),
         name="line_correlate",
     )
-    return call(records, alive.reshape(1, C), offsets, forward_table(), lag_table())
+    return call(records, alive.reshape(1, C), offsets, tables())
 
 
 def solution(mesh):

time: 57.5 us -> 55 us (0.957); the launches traced: 56.7 us -> 54.9 us
  Pallas kernels: 55 us -> 53.5 us
    pallas_call x1, Pallas kernels: 55 us -> 53.5 us  [shards(): return call(records, alive.reshape(1, C), offsets, tables())]
    unnamed x1 -> x5, local copies, waits for them, and re-layouts: 1.67 us -> 1.4 us
where the time goes in v4:
time: 55 us; the launch traced here: 54.9 us
  Pallas kernels  53.5 us (97%)
  local copies, waits for them, and re-layouts  1.4 us (3%)
    pallas_call x1, Pallas kernels, shards(): return call(records, alive.reshape(1, C), offsets, tables())  53.5 us
    unnamed x5, local copies, waits for them, and re-layouts  1.4 us

profile of v4, /device:TPU:1, one launch (start us, length us, event | category | flops | bytes accessed | tf_op | source)
XLA Modules:
  0.0 54.9 jit_solution(16196328115254266466)
XLA Ops:
  0.0 0.0 copy-start.1
  0.0 0.0 copy-start
  0.0 0.7 %copy-done.1 = s32[1,16]{1,0:T(1,128)S(1)} copy-done((s32[1,16]{1,0:T(1,128)S(1)}, s32[1,16]{1,0:T(1,128)}, u32[]{:S(2)}) %copy-start.1) | copy-done | bytes 88
  0.7 0.0 copy-done
  0.7 53.5 %line_correlate.1 = bf16[2,256,256]{2,1,0:T(8,128)(2,1)S(1)} custom-call(bf16[1,256,4,512]{3,2,1,0:T(4,128)(2,1)} %rec_hbm.1, s32[1,256]{1,0:T(1,128)S(1)} %bitcast.1, s32[1,16]{1,0:T(1,128)S(1)} %copy-done.1, f32[256,768]{1,0:T(8,128)} %constant.2.clone.tab_hbm), custom_call_target="tpu_custom_call" | custom-call | flops 400000000 | bytes 3000000 | tf_op jit(solution)/shard_map/line_correlate/pallas_call | solution.py:361
  54.2 0.7 %copy.6 = bf16[2,256,256]{2,1,0:T(8,128)(2,1)} copy(bf16[2,256,256]{2,1,0:T(8,128)(2,1)S(1)} %line_correlate.1) | data formatting | bytes 524288
Async XLA Ops:
  0.0 0.7 %copy-start.1 = (s32[1,16]{1,0:T(1,128)S(1)}, s32[1,16]{1,0:T(1,128)}, u32[]{:S(2)}) copy-start(s32[1,16]{1,0:T(1,128)} %off_hbm.1) | copy-start | bytes 196
  0.0 0.7 %copy-start = (s32[256]{0:T(256)S(1)}, s32[256]{0:T(256)}, u32[]{:S(2)}) copy-start(s32[256]{0:T(256)} %param.5) | copy-start | bytes 3076

commit v5 on v4

--- a/solution.py
+++ b/solution.py
@@ -79,6 +79,10 @@
     def on_chain(link):
         return (((link // 2) * 2 + zh) * 2 + link % 2, seg)
 
+    loads = [pltpu.make_async_copy(source, target, load_sem.at[i]) for i, (source, target) in enumerate((
+        (rec_hbm, rec_ref), (tab_hbm, tab_ref), (alive_hbm, alive_ref), (off_hbm, off_ref)))]
+    for load in loads:
+        load.start()
     barrier = pltpu.get_barrier_semaphore()
 
     for s in range(SEGS):
@@ -90,10 +94,6 @@
                 pl.semaphore_signal(barrier, 1, device_id=sender, device_id_type=MESH)
     pl.semaphore_signal(barrier, 1, device_id=on_chain(after), device_id_type=MESH)
 
-    loads = [pltpu.make_async_copy(source, target, load_sem.at[i]) for i, (source, target) in enumerate((
-        (rec_hbm, rec_ref), (tab_hbm, tab_ref), (alive_hbm, alive_ref), (off_hbm, off_ref)))]
-    for load in loads:
-        load.start()
     for load in loads:
         load.wait()
     off_src[...] = jnp.zeros_like(off_src)
@@ -229,10 +229,15 @@
                 s = chip % SEGS
                 white_wait(phase, 0, s)
                 rim_copy(phase, s).start()
-                white_wait(phase, 1, s)
             return 0
 
         lax.fori_loop(0, CHIPS, arrive, 0)
+
+        def arrive_more(s, _):
+            white_wait(phase, 1, s)
+            return 0
+
+        lax.fori_loop(0, SEGS, arrive_more, 0)
         for block in range(2):
             for part in range(2):
                 flipped = transposed(recv[phase, block, part])

time: 55 us -> 55.1 us (level)
  no operation moved by 1% of the time
where the time goes in v5:
time: 55.1 us; the launch traced here: 54.9 us
  Pallas kernels  53.5 us (97%)
  local copies, waits for them, and re-layouts  1.4 us (3%)
    pallas_call x1, Pallas kernels, shards(): return call(records, alive.reshape(1, C), offsets, tables())  53.5 us
    unnamed x5, local copies, waits for them, and re-layouts  1.4 us

profile of v5, /device:TPU:1, one launch (start us, length us, event | category | flops | bytes accessed | tf_op | source)
XLA Modules:
  0.0 54.9 jit_solution(16721966341534016422)
XLA Ops:
  0.0 0.0 copy-start.1
  0.0 0.0 copy-start
  0.0 0.7 %copy-done.1 = s32[1,16]{1,0:T(1,128)S(1)} copy-done((s32[1,16]{1,0:T(1,128)S(1)}, s32[1,16]{1,0:T(1,128)}, u32[]{:S(2)}) %copy-start.1) | copy-done | bytes 88
  0.7 0.0 copy-done
  0.7 53.5 %line_correlate.1 = bf16[2,256,256]{2,1,0:T(8,128)(2,1)S(1)} custom-call(bf16[1,256,4,512]{3,2,1,0:T(4,128)(2,1)} %rec_hbm.1, s32[1,256]{1,0:T(1,128)S(1)} %bitcast.1, s32[1,16]{1,0:T(1,128)S(1)} %copy-done.1, f32[256,768]{1,0:T(8,128)} %constant.2.clone.tab_hbm), custom_call_target="tpu_custom_call" | custom-call | flops 400000000 | bytes 3000000 | tf_op jit(solution)/shard_map/line_correlate/pallas_call | solution.py:366
  54.2 0.7 %copy.6 = bf16[2,256,256]{2,1,0:T(8,128)(2,1)} copy(bf16[2,256,256]{2,1,0:T(8,128)(2,1)S(1)} %line_correlate.1) | data formatting | bytes 524288
Async XLA Ops:
  0.0 0.7 %copy-start.1 = (s32[1,16]{1,0:T(1,128)S(1)}, s32[1,16]{1,0:T(1,128)}, u32[]{:S(2)}) copy-start(s32[1,16]{1,0:T(1,128)} %off_hbm.1) | copy-start | bytes 196
  0.0 0.7 %copy-start = (s32[256]{0:T(256)S(1)}, s32[256]{0:T(256)}, u32[]{:S(2)}) copy-start(s32[256]{0:T(256)} %param.5) | copy-start | bytes 3076
